TPU v7x, 512 devices: a whole 4x8x8 slice. The times are simulated.
512 devices in a mesh: ctx: 128 (over y_lo, x, z), mp: 4 (over y_hi, core).
Axes of the slice: x: 4, y: 8 (y_hi: 2, y_lo: 4; y = y_hi * 4 + y_lo), z: 8, core: 2. Of those that a mesh axis runs over, the one named last changes fastest.
Arguments:
- query_rows: bfloat16 [16384, 2048], P('ctx', 'mp'), may hold values from -51 to 51
- key_rows: bfloat16 [16384, 2048], P('ctx', 'mp'), may hold values from -4 to 4
- value_rows: bfloat16 [16384, 2048], P('ctx', 'mp'), may hold values from -6 to 6
- inputs: bfloat16 [16384, 2048], P('ctx', 'mp'), may hold values from -3 to 3
- out_weight: bfloat16 [2048, 2048], P('mp'), may hold values from -0.125 to 0.125
- kernel: float32 [31, 2048], P(None, 'mp'), may hold values from -1 to 1
- cotangent: bfloat16 [16384, 2048], P('ctx', 'mp'), may hold values from -6 to 6
Outputs:
- output: bfloat16 [16384, 2048], P('ctx', 'mp')
- grad_input: bfloat16 [16384, 2048], P('ctx', 'mp')
- grad_query: bfloat16 [16384, 2048], P('ctx', 'mp')
- grad_key: bfloat16 [16384, 2048], P('ctx', 'mp')
- grad_value: bfloat16 [16384, 2048], P('ctx', 'mp')
All inputs are finite; a program needn't handle non-finite values.
Results may differ from a plain program's by a relative error of at most 0.024.
Values may be sent and summed in bfloat16 or wider, within the bound.
A program may use at most 64 MiB of HBM per device.

v0:
```python
import math
import jax
import jax.numpy as jnp
from jax import lax
from jax.sharding import PartitionSpec as P

HDIM = 128
LOOK = 2


def shifted(block, axis, distance):
    devices = range(lax.axis_size(axis))
    route = [(i - distance, i) for i in devices if i - distance in devices]
    return lax.ppermute(block, axis, route)


def with_halo(block, sides, width):
    for axis, dim in sides:
        count = lax.axis_size(axis)
        forward = [(i, i + 1) for i in range(count - 1)]
        backward = [(target, source) for source, target in forward]
        low = lax.ppermute(
            lax.slice_in_dim(block, block.shape[dim] - width, None, axis=dim), axis, forward
        )
        high = lax.ppermute(lax.slice_in_dim(block, 0, width, axis=dim), axis, backward)
        block = jnp.concatenate([low, block, high], axis=dim)
    return block


def kv_move(kv_pair, offset):
    return shifted(kv_pair, "ctx", offset)


def grad_move(part_pair, offset):
    return shifted(part_pair.astype(jnp.bfloat16), "ctx", offset).astype(part_pair.dtype)


def conv_rim(field_rows, rim_width):
    return with_halo(field_rows, (("ctx", 0),), rim_width)


def relay_window(center, move_step):
    lower_list = []
    upper_list = []
    rising = center
    falling = center
    for offset in range(LOOK):
        rising = move_step(rising, 1)
        falling = move_step(falling, -1)
        lower_list.append(rising)
        upper_list.append(falling)
    return lower_list[::-1] + [center] + upper_list


def per_device(query_rows, key_rows, value_rows, inputs, out_weight, kernel, cotangent):
    frames, local_width = query_rows.shape
    local_heads = local_width // HDIM
    score_scale = 1.0 / math.sqrt(HDIM)
    window_len = (2 * LOOK + 1) * frames
    dev_index = lax.axis_index("ctx")
    dev_count = lax.axis_size("ctx")
    owners = dev_index + jnp.arange(window_len, dtype=jnp.int32) // frames - LOOK
    in_range = (owners >= 0) & (owners < dev_count)
    kv_center = jnp.stack([key_rows, value_rows])
    kv_blocks = relay_window(kv_center, kv_move)
    kv_window = jnp.concatenate(kv_blocks, axis=1)
    key_win = kv_window[0].reshape(window_len, local_heads, HDIM)
    value_win = kv_window[1].reshape(window_len, local_heads, HDIM)
    query_heads = query_rows.reshape(frames, local_heads, HDIM)
    scores = (
        jnp.einsum("qhd,khd->hqk", query_heads, key_win, preferred_element_type=jnp.float32)
        * score_scale
    )
    scores = jnp.where(in_range[None, None, :], scores, -jnp.inf)
    row_max = jnp.max(scores, axis=2)
    log_total = row_max + jnp.log(jnp.sum(jnp.exp(scores - row_max[:, :, None]), axis=2))
    attn_probs = jnp.exp(scores - log_total[:, :, None])
    probs_low = attn_probs.astype(jnp.bfloat16)
    attended = jnp.einsum(
        "hqk,khd->qhd", probs_low, value_win, preferred_element_type=jnp.float32
    ).astype(jnp.bfloat16)
    attended_flat = attended.reshape(frames, local_width)
    partial_out = jnp.dot(attended_flat, out_weight, preferred_element_type=jnp.float32)
    mixed = lax.psum_scatter(
        partial_out.astype(jnp.bfloat16), "mp", scatter_dimension=1, tiled=True
    ).astype(jnp.float32)
    hidden = (inputs.astype(jnp.float32) + mixed).astype(jnp.bfloat16)
    taps = kernel.shape[0]
    half_kernel = taps // 2
    hidden_pad = conv_rim(hidden, half_kernel).astype(jnp.float32)
    conv_out = jnp.zeros((frames, local_width), jnp.float32)
    for tap_index in range(taps):
        conv_out = (
            conv_out + kernel[tap_index][None, :] * hidden_pad[tap_index : tap_index + frames]
        )
    conv_gate = jax.nn.sigmoid(conv_out)
    output = (hidden.astype(jnp.float32) + conv_out * conv_gate).astype(jnp.bfloat16)
    grad_conv = (
        cotangent.astype(jnp.float32) * (conv_gate + conv_out * conv_gate * (1.0 - conv_gate))
    ).astype(jnp.bfloat16)
    grad_pad = conv_rim(grad_conv, half_kernel).astype(jnp.float32)
    grad_hidden = cotangent.astype(jnp.float32)
    for tap_index in range(taps):
        first_row = 2 * half_kernel - tap_index
        grad_hidden = (
            grad_hidden + kernel[tap_index][None, :] * grad_pad[first_row : first_row + frames]
        )
    grad_input = grad_hidden.astype(jnp.bfloat16)
    upstream = jnp.einsum(
        "rn,wn->rw",
        lax.all_gather(grad_input, "mp", axis=1, tiled=True),
        out_weight,
        preferred_element_type=jnp.float32,
    ).astype(jnp.bfloat16)
    up_heads = upstream.reshape(frames, local_heads, HDIM)
    row_delta = jnp.sum(up_heads.astype(jnp.float32) * attended.astype(jnp.float32), axis=2).T
    grad_dots = jnp.einsum("qhd,khd->hqk", up_heads, value_win, preferred_element_type=jnp.float32)
    grad_scores = (attn_probs * (grad_dots - row_delta[:, :, None]) * score_scale).astype(
        jnp.bfloat16
    )
    grad_query = jnp.einsum(
        "hqk,khd->qhd", grad_scores, key_win, preferred_element_type=jnp.float32
    )
    grad_query = grad_query.astype(jnp.bfloat16).reshape(frames, local_width)
    key_parts = jnp.einsum(
        "hqk,qhd->khd", grad_scores, query_heads, preferred_element_type=jnp.float32
    )
    value_parts = jnp.einsum(
        "hqk,qhd->khd", probs_low, up_heads, preferred_element_type=jnp.float32
    )
    part_stack = jnp.stack(
        [key_parts.reshape(window_len, local_width), value_parts.reshape(window_len, local_width)]
    )

    def part_block(position):
        return part_stack[:, position * frames : (position + 1) * frames]

    rising = part_block(2 * LOOK)
    offset = 1
    rising = grad_move(rising, 1) + part_block(LOOK + offset)
    rising = grad_move(rising, 1)
    falling = part_block(0)
    offset = 1
    falling = grad_move(falling, -1) + part_block(LOOK - offset)
    falling = grad_move(falling, -1)
    key_sums = part_block(LOOK) + rising + falling
    grad_key = key_sums[0].astype(jnp.bfloat16)
    grad_value = key_sums[1].astype(jnp.bfloat16)
    return (output, grad_input, grad_query, grad_key, grad_value)


def solution(mesh):
    placed = (
        P("ctx", "mp"),
        P("ctx", "mp"),
        P("ctx", "mp"),
        P("ctx", "mp"),
        P("mp", None),
        P(None, "mp"),
        P("ctx", "mp"),
    )
    return jax.shard_map(
        per_device,
        mesh=mesh,
        in_specs=placed,
        out_specs=(P("ctx", "mp"), P("ctx", "mp"), P("ctx", "mp"), P("ctx", "mp"), P("ctx", "mp")),
        check_vma=False,
    )
```

profile of v0, /device:TPU:8, one launch (start us, length us, event | category | flops | bytes accessed | tf_op | source)
XLA Modules:
  0.0 188.9 jit_solution(1581389626179336944)
XLA Ops:
  9.5 4.3 %collective-permute-start = (bf16[2,128,512]{1,2,0:T(8,128)(2,1)S(1)}, bf16[2,128,512]{1,2,0:T(8,128)(2,1)S(1)}, u32[]{:S(2)}, u32[]{:S(2)}) collective-permute-start(bf16[2,128,512]{1,2,0:T(8,128)(2,1)S(1)} %pad_maximum_fusion.1), channel_id=1, source_target_pairs={{0,4},{4,8},{8,12},{12,16},{16,20},{20,24},{24,28},{28,32},{32,36}... | collective-permute-start | bytes 786440 | tf_op jit(solution)/shard_map/ppermute | solution.py:14
  13.7 10.7 %collective-permute-start.2 = (bf16[2,128,512]{1,2,0:T(8,128)(2,1)S(1)}, bf16[2,128,512]{1,2,0:T(8,128)(2,1)S(1)}, u32[]{:S(2)}, u32[]{:S(2)}) collective-permute-start(bf16[2,128,512]{1,2,0:T(8,128)(2,1)S(1)} %pad_maximum_fusion.1), channel_id=1, source_target_pairs={{4,0},{8,4},{12,8},{16,12},{20,16},{24,20},{28,24},{32,28},{36,32}... | collective-permute-start | bytes 786440 | tf_op jit(solution)/shard_map/ppermute | solution.py:14
  24.4 4.4 %collective-permute-done = bf16[2,128,512]{1,2,0:T(8,128)(2,1)S(1)} collective-permute-done((bf16[2,128,512]{1,2,0:T(8,128)(2,1)S(1)}, bf16[2,128,512]{1,2,0:T(8,128)(2,1)S(1)}, u32[]{:S(2)}, u32[]{:S(2)}) %collective-permute-start) | collective-permute-done | bytes 262176 | tf_op jit(solution)/shard_map/ppermute | solution.py:14
  28.8 1.9 %collective-permute-start.1 = (bf16[2,128,512]{1,2,0:T(8,128)(2,1)S(1)}, bf16[2,128,512]{1,2,0:T(8,128)(2,1)S(1)}, u32[]{:S(2)}, u32[]{:S(2)}) collective-permute-start(bf16[2,128,512]{1,2,0:T(8,128)(2,1)S(1)} %collective-permute-done), channel_id=1, source_target_pairs={{0,4},{4,8},{8,12},{12,16},{16,20},{20,24},{24,28},{28,32},{32,36}... | collective-permute-start | bytes 786440 | tf_op jit(solution)/shard_map/ppermute | solution.py:14
  31.8 8.1 %collective-permute-start.3 = (bf16[2,128,512]{1,2,0:T(8,128)(2,1)S(1)}, bf16[2,128,512]{1,2,0:T(8,128)(2,1)S(1)}, u32[]{:S(2)}, u32[]{:S(2)}) collective-permute-start(bf16[2,128,512]{1,2,0:T(8,128)(2,1)S(1)} %collective-permute-done.2), channel_id=1, source_target_pairs={{4,0},{8,4},{12,8},{16,12},{20,16},{24,20},{28,24},{32,28},{36,32}... | collective-permute-start | bytes 786440 | tf_op jit(solution)/shard_map/ppermute | solution.py:14
  39.9 2.5 %collective-permute-done.1 = bf16[2,128,512]{1,2,0:T(8,128)(2,1)S(1)} collective-permute-done((bf16[2,128,512]{1,2,0:T(8,128)(2,1)S(1)}, bf16[2,128,512]{1,2,0:T(8,128)(2,1)S(1)}, u32[]{:S(2)}, u32[]{:S(2)}) %collective-permute-start.1) | collective-permute-done | bytes 262176 | tf_op jit(solution)/shard_map/ppermute | solution.py:14
  42.6 2.0 %collective-permute-done.3 = bf16[2,128,512]{1,2,0:T(8,128)(2,1)S(1)} collective-permute-done((bf16[2,128,512]{1,2,0:T(8,128)(2,1)S(1)}, bf16[2,128,512]{1,2,0:T(8,128)(2,1)S(1)}, u32[]{:S(2)}, u32[]{:S(2)}) %collective-permute-start.3) | collective-permute-done | bytes 262176 | tf_op jit(solution)/shard_map/ppermute | solution.py:14
  46.9 1.3 convolution_convert_fusion
  48.2 1.8 fusion.96
  50.0 41.9 %reduce-scatter.2.cloned.1.call-done = bf16[128,512]{1,0:T(8,128)(2,1)} async-done(((bf16[128,2048]{1,0:T(8,128)(2,1)}), bf16[128,512]{1,0:T(8,128)(2,1)}) %reduce-scatter.2.cloned.1.call-update) | async-done | bytes 131088 | tf_op jit(solution)/shard_map/reduce_scatter | solution.py:84
  93.0 3.6 %collective-permute-start.4 = (bf16[15,512]{1,0:T(8,128)(2,1)S(1)}, bf16[15,512]{1,0:T(8,128)(2,1)S(1)}, u32[]{:S(2)}, u32[]{:S(2)}) collective-permute-start(bf16[15,512]{1,0:T(8,128)(2,1)S(1)} %get-tuple-element.27), channel_id=1, source_target_pairs={{0,4},{4,8},{8,12},{12,16},{16,20},{20,24},{24,28},{28,32},{32,36}... | collective-permute-start | bytes 46088 | tf_op jit(solution)/shard_map/ppermute | solution.py:22
  96.5 6.5 %collective-permute-start.5 = (bf16[15,512]{1,0:T(8,128)(2,1)S(1)}, bf16[15,512]{1,0:T(8,128)(2,1)S(1)}, u32[]{:S(2)}, u32[]{:S(2)}) collective-permute-start(bf16[15,512]{1,0:T(8,128)(2,1)S(1)} %get-tuple-element.28), channel_id=1, source_target_pairs={{4,0},{8,4},{12,8},{16,12},{20,16},{24,20},{28,24},{32,28},{36,32}... | collective-permute-start | bytes 46088 | tf_op jit(solution)/shard_map/ppermute | solution.py:25
  104.7 2.3 %fusion.17 = (bf16[128,512]{1,0:T(8,128)(2,1)S(1)}, f32[128,512]{1,0:T(8,128)}) fusion(bf16[128,512]{1,0:T(8,128)(2,1)S(1)} %copy-done.14, f32[158,512]{1,0:T(8,128)S(1)} %maximum_convert_fusion, f32[512]{0:T(512)S(1)} %bitcast.146, f32[512]{0:T(512)S(1)} %bitcast.148, f32[512]{0:T(512)S(1)} %bitcast.90, f32[512]{0:T(512)S(1)} %bitcast.92, f32[512]{0:T(512)} %bitcast.94, ...), kind=kLoop, calls=%fused_computation.34 | loop fusion | flops 4653056 | bytes 8714240 | tf_op jit(solution)/shard_map/convert_element_type | solution.py:100
  107.0 1.9 %collective-permute-start.6 = (bf16[15,512]{1,0:T(8,128)(2,1)S(1)}, bf16[15,512]{1,0:T(8,128)(2,1)S(1)}, u32[]{:S(2)}, u32[]{:S(2)}) collective-permute-start(bf16[15,512]{1,0:T(8,128)(2,1)S(1)} %get-tuple-element.25), channel_id=1, source_target_pairs={{0,4},{4,8},{8,12},{12,16},{16,20},{20,24},{24,28},{28,32},{32,36}... | collective-permute-start | bytes 46088 | tf_op jit(solution)/shard_map/ppermute | solution.py:22
  108.9 8.4 %collective-permute-start.7 = (bf16[15,512]{1,0:T(8,128)(2,1)S(1)}, bf16[15,512]{1,0:T(8,128)(2,1)S(1)}, u32[]{:S(2)}, u32[]{:S(2)}) collective-permute-start(bf16[15,512]{1,0:T(8,128)(2,1)S(1)} %get-tuple-element.26), channel_id=1, source_target_pairs={{4,0},{8,4},{12,8},{16,12},{20,16},{24,20},{28,24},{32,28},{36,32}... | collective-permute-start | bytes 46088 | tf_op jit(solution)/shard_map/ppermute | solution.py:25
  117.3 1.4 collective-permute-done.7
  119.8 11.3 %all_gather.3 = bf16[128,2048]{1,0:T(8,128)(2,1)S(1)} all-gather(bf16[128,512]{1,0:T(8,128)(2,1)S(1)} %fusion.44), channel_id=1, replica_groups=mesh['ctx'=128,'mp'=4] {'mp'}, dimensions={1}, use_global_device_ids=true | all-gather | bytes 655360 | tf_op jit(solution)/shard_map/all_gather | solution.py:111
  131.1 1.5 convolution_convert_fusion.1
  134.6 1.5 fusion.80
  136.0 1.3 fusion.5
  137.4 1.7 copy.41
  139.1 2.5 %fusion.99 = f32[4,640,128]{1,2,0:T(8,128)} fusion(bf16[4,128,640]{1,2,0:T(8,128)(2,1)} %fusion.5, bf16[128,4,128]{0,2,1:T(8,128)(2,1)S(1)} %bitcast.81), kind=kOutput, calls=%fused_computation.194 | convolution fusion | flops 83886080 | bytes 2097152 | tf_op jit(solution)/shard_map/hqk,qhd->khd/dot_general | solution.py:125
  141.7 2.8 %copy.40 = f32[1,640,512]{2,1,0:T(8,128)} copy(f32[1,640,512]{1,2,0:T(8,128)} %bitcast.77) | data formatting | bytes 2621440 | tf_op jit(solution)/shard_map/stack;reshape | solution.py:131
  144.5 1.6 fusion
  146.2 1.9 %collective-permute-start.8 = (bf16[2,128,512]{2,1,0:T(8,128)(2,1)S(1)}, bf16[2,128,512]{2,1,0:T(8,128)(2,1)S(1)}, u32[]{:S(2)}, u32[]{:S(2)}) collective-permute-start(bf16[2,128,512]{2,1,0:T(8,128)(2,1)S(1)} %get-tuple-element.19), channel_id=1, source_target_pairs={{0,4},{4,8},{8,12},{12,16},{16,20},{20,24},{24,28},{28,32},{32,36}... | collective-permute-start | bytes 786440 | tf_op jit(solution)/shard_map/ppermute | solution.py:14
  148.1 8.8 %collective-permute-start.10 = (bf16[2,128,512]{2,1,0:T(8,128)(2,1)S(1)}, bf16[2,128,512]{2,1,0:T(8,128)(2,1)S(1)}, u32[]{:S(2)}, u32[]{:S(2)}) collective-permute-start(bf16[2,128,512]{2,1,0:T(8,128)(2,1)S(1)} %get-tuple-element.20), channel_id=1, source_target_pairs={{4,0},{8,4},{12,8},{16,12},{20,16},{24,20},{28,24},{32,28},{36,32}... | collective-permute-start | bytes 786440 | tf_op jit(solution)/shard_map/ppermute | solution.py:14
  157.0 4.7 %collective-permute-done.8 = bf16[2,128,512]{2,1,0:T(8,128)(2,1)S(1)} collective-permute-done((bf16[2,128,512]{2,1,0:T(8,128)(2,1)S(1)}, bf16[2,128,512]{2,1,0:T(8,128)(2,1)S(1)}, u32[]{:S(2)}, u32[]{:S(2)}) %collective-permute-start.8) | collective-permute-done | bytes 262176 | tf_op jit(solution)/shard_map/ppermute | solution.py:14
  161.7 1.4 collective-permute-done.10
  164.0 1.9 %collective-permute-start.9 = (bf16[2,128,512]{2,1,0:T(8,128)(2,1)}, bf16[2,128,512]{2,1,0:T(8,128)(2,1)}, u32[]{:S(2)}, u32[]{:S(2)}) collective-permute-start(bf16[2,128,512]{2,1,0:T(8,128)(2,1)} %get-tuple-element.17), channel_id=1, source_target_pairs={{0,4},{4,8},{8,12},{12,16},{16,20},{20,24},{24,28},{28,32},{32,36}... | collective-permute-start | bytes 786440 | tf_op jit(solution)/shard_map/ppermute | solution.py:14
  165.9 8.6 %collective-permute-start.11 = (bf16[2,128,512]{2,1,0:T(8,128)(2,1)}, bf16[2,128,512]{2,1,0:T(8,128)(2,1)}, u32[]{:S(2)}, u32[]{:S(2)}) collective-permute-start(bf16[2,128,512]{2,1,0:T(8,128)(2,1)} %get-tuple-element.18), channel_id=1, source_target_pairs={{4,0},{8,4},{12,8},{16,12},{20,16},{24,20},{28,24},{32,28},{36,32}... | collective-permute-start | bytes 786440 | tf_op jit(solution)/shard_map/ppermute | solution.py:14
  176.4 2.5 %collective-permute-done.9 = bf16[2,128,512]{2,1,0:T(8,128)(2,1)} collective-permute-done((bf16[2,128,512]{2,1,0:T(8,128)(2,1)}, bf16[2,128,512]{2,1,0:T(8,128)(2,1)}, u32[]{:S(2)}, u32[]{:S(2)}) %collective-permute-start.9) | collective-permute-done | bytes 262176 | tf_op jit(solution)/shard_map/ppermute | solution.py:14
  180.1 1.2 fusion.10
  (99 shorter events, 15.9 us)
Async XLA Ops:
  7.2 39.7 %copy-start = (bf16[512,2048]{1,0:T(8,128)(2,1)S(1)}, bf16[512,2048]{1,0:T(8,128)(2,1)}, u32[]{:S(2)}) copy-start(bf16[512,2048]{1,0:T(8,128)(2,1)} %param.11) | copy-start | bytes 6291460
  7.2 84.8 %reduce-scatter.2.cloned.1.call-start = ((), (), s32[]{:S(2)}) async-start(), calls=%async_computation.1 | async-start | bytes 655360 | tf_op jit(solution)/shard_map/reduce_scatter | solution.py:84
  9.5 19.3 %collective-permute-start = (bf16[2,128,512]{1,2,0:T(8,128)(2,1)S(1)}, bf16[2,128,512]{1,2,0:T(8,128)(2,1)S(1)}, u32[]{:S(2)}, u32[]{:S(2)}) collective-permute-start(bf16[2,128,512]{1,2,0:T(8,128)(2,1)S(1)} %pad_maximum_fusion.1), channel_id=1, source_target_pairs={{0,4},{4,8},{8,12},{12,16},{16,20},{20,24},{24,28},{28,32},{32,36}... | collective-permute-start | bytes 786440 | tf_op jit(solution)/shard_map/ppermute | solution.py:14
  13.7 18.0 %collective-permute-start.2 = (bf16[2,128,512]{1,2,0:T(8,128)(2,1)S(1)}, bf16[2,128,512]{1,2,0:T(8,128)(2,1)S(1)}, u32[]{:S(2)}, u32[]{:S(2)}) collective-permute-start(bf16[2,128,512]{1,2,0:T(8,128)(2,1)S(1)} %pad_maximum_fusion.1), channel_id=1, source_target_pairs={{4,0},{8,4},{12,8},{16,12},{20,16},{24,20},{28,24},{32,28},{36,32}... | collective-permute-start | bytes 786440 | tf_op jit(solution)/shard_map/ppermute | solution.py:14
  28.8 13.6 %collective-permute-start.1 = (bf16[2,128,512]{1,2,0:T(8,128)(2,1)S(1)}, bf16[2,128,512]{1,2,0:T(8,128)(2,1)S(1)}, u32[]{:S(2)}, u32[]{:S(2)}) collective-permute-start(bf16[2,128,512]{1,2,0:T(8,128)(2,1)S(1)} %collective-permute-done), channel_id=1, source_target_pairs={{0,4},{4,8},{8,12},{12,16},{16,20},{20,24},{24,28},{28,32},{32,36}... | collective-permute-start | bytes 786440 | tf_op jit(solution)/shard_map/ppermute | solution.py:14
  31.8 12.9 %collective-permute-start.3 = (bf16[2,128,512]{1,2,0:T(8,128)(2,1)S(1)}, bf16[2,128,512]{1,2,0:T(8,128)(2,1)S(1)}, u32[]{:S(2)}, u32[]{:S(2)}) collective-permute-start(bf16[2,128,512]{1,2,0:T(8,128)(2,1)S(1)} %collective-permute-done.2), channel_id=1, source_target_pairs={{4,0},{8,4},{12,8},{16,12},{20,16},{24,20},{28,24},{32,28},{36,32}... | collective-permute-start | bytes 786440 | tf_op jit(solution)/shard_map/ppermute | solution.py:14
  48.2 56.3 %copy-start.14 = (bf16[128,512]{1,0:T(8,128)(2,1)S(1)}, bf16[128,512]{1,0:T(8,128)(2,1)}, u32[]{:S(2)}) copy-start(bf16[128,512]{1,0:T(8,128)(2,1)} %param.13) | copy-start | bytes 393220
  93.0 11.1 %collective-permute-start.4 = (bf16[15,512]{1,0:T(8,128)(2,1)S(1)}, bf16[15,512]{1,0:T(8,128)(2,1)S(1)}, u32[]{:S(2)}, u32[]{:S(2)}) collective-permute-start(bf16[15,512]{1,0:T(8,128)(2,1)S(1)} %get-tuple-element.27), channel_id=1, source_target_pairs={{0,4},{4,8},{8,12},{12,16},{16,20},{20,24},{24,28},{28,32},{32,36}... | collective-permute-start | bytes 46088 | tf_op jit(solution)/shard_map/ppermute | solution.py:22
  96.5 7.9 %collective-permute-start.5 = (bf16[15,512]{1,0:T(8,128)(2,1)S(1)}, bf16[15,512]{1,0:T(8,128)(2,1)S(1)}, u32[]{:S(2)}, u32[]{:S(2)}) collective-permute-start(bf16[15,512]{1,0:T(8,128)(2,1)S(1)} %get-tuple-element.28), channel_id=1, source_target_pairs={{4,0},{8,4},{12,8},{16,12},{20,16},{24,20},{28,24},{32,28},{36,32}... | collective-permute-start | bytes 46088 | tf_op jit(solution)/shard_map/ppermute | solution.py:25
  104.5 14.3 %copy-start.15 = (f32[1,512]{1,0:T(1,128)S(1)}, f32[1,512]{1,0:T(1,128)}, u32[]{:S(2)}) copy-start(f32[1,512]{1,0:T(1,128)} %get-tuple-element.32) | copy-start | bytes 6148
  104.5 14.3 %copy-start.16 = (f32[1,512]{1,0:T(1,128)S(1)}, f32[1,512]{1,0:T(1,128)}, u32[]{:S(2)}) copy-start(f32[1,512]{1,0:T(1,128)} %get-tuple-element.33) | copy-start | bytes 6148
  104.6 14.3 %copy-start.17 = (f32[1,512]{1,0:T(1,128)S(1)}, f32[1,512]{1,0:T(1,128)}, u32[]{:S(2)}) copy-start(f32[1,512]{1,0:T(1,128)} %get-tuple-element.34) | copy-start | bytes 6148
  104.6 14.3 %copy-start.18 = (f32[1,512]{1,0:T(1,128)S(1)}, f32[1,512]{1,0:T(1,128)}, u32[]{:S(2)}) copy-start(f32[1,512]{1,0:T(1,128)} %get-tuple-element.35) | copy-start | bytes 6148
  104.6 14.3 %copy-start.19 = (f32[1,512]{1,0:T(1,128)S(1)}, f32[1,512]{1,0:T(1,128)}, u32[]{:S(2)}) copy-start(f32[1,512]{1,0:T(1,128)} %get-tuple-element.36) | copy-start | bytes 6148
  104.6 14.3 %copy-start.20 = (f32[1,512]{1,0:T(1,128)S(1)}, f32[1,512]{1,0:T(1,128)}, u32[]{:S(2)}) copy-start(f32[1,512]{1,0:T(1,128)} %get-tuple-element.37) | copy-start | bytes 6148
  104.6 14.3 %copy-start.21 = (f32[1,512]{1,0:T(1,128)S(1)}, f32[1,512]{1,0:T(1,128)}, u32[]{:S(2)}) copy-start(f32[1,512]{1,0:T(1,128)} %get-tuple-element.38) | copy-start | bytes 6148
  104.6 14.3 %copy-start.22 = (f32[1,512]{1,0:T(1,128)S(1)}, f32[1,512]{1,0:T(1,128)}, u32[]{:S(2)}) copy-start(f32[1,512]{1,0:T(1,128)} %get-tuple-element.39) | copy-start | bytes 6148
  104.6 14.3 %copy-start.23 = (f32[1,512]{1,0:T(1,128)S(1)}, f32[1,512]{1,0:T(1,128)}, u32[]{:S(2)}) copy-start(f32[1,512]{1,0:T(1,128)} %get-tuple-element.40) | copy-start | bytes 6148
  104.6 14.3 %copy-start.24 = (f32[1,512]{1,0:T(1,128)S(1)}, f32[1,512]{1,0:T(1,128)}, u32[]{:S(2)}) copy-start(f32[1,512]{1,0:T(1,128)} %get-tuple-element.41) | copy-start | bytes 6148
  104.6 14.3 %copy-start.25 = (f32[1,512]{1,0:T(1,128)S(1)}, f32[1,512]{1,0:T(1,128)}, u32[]{:S(2)}) copy-start(f32[1,512]{1,0:T(1,128)} %get-tuple-element.42) | copy-start | bytes 6148
  104.6 14.3 %copy-start.26 = (f32[1,512]{1,0:T(1,128)S(1)}, f32[1,512]{1,0:T(1,128)}, u32[]{:S(2)}) copy-start(f32[1,512]{1,0:T(1,128)} %get-tuple-element.43) | copy-start | bytes 6148
  107.0 10.4 %collective-permute-start.6 = (bf16[15,512]{1,0:T(8,128)(2,1)S(1)}, bf16[15,512]{1,0:T(8,128)(2,1)S(1)}, u32[]{:S(2)}, u32[]{:S(2)}) collective-permute-start(bf16[15,512]{1,0:T(8,128)(2,1)S(1)} %get-tuple-element.25), channel_id=1, source_target_pairs={{0,4},{4,8},{8,12},{12,16},{16,20},{20,24},{24,28},{28,32},{32,36}... | collective-permute-start | bytes 46088 | tf_op jit(solution)/shard_map/ppermute | solution.py:22
  108.9 9.9 %collective-permute-start.7 = (bf16[15,512]{1,0:T(8,128)(2,1)S(1)}, bf16[15,512]{1,0:T(8,128)(2,1)S(1)}, u32[]{:S(2)}, u32[]{:S(2)}) collective-permute-start(bf16[15,512]{1,0:T(8,128)(2,1)S(1)} %get-tuple-element.26), channel_id=1, source_target_pairs={{4,0},{8,4},{12,8},{16,12},{20,16},{24,20},{28,24},{32,28},{36,32}... | collective-permute-start | bytes 46088 | tf_op jit(solution)/shard_map/ppermute | solution.py:25
  144.5 18.6 %copy-start.1 = (f32[1,640,512]{2,1,0:T(8,128)S(1)}, f32[1,640,512]{2,1,0:T(8,128)}, u32[]{:S(2)}) copy-start(f32[1,640,512]{2,1,0:T(8,128)} %copy.40) | copy-start | bytes 3932164
  146.2 15.5 %collective-permute-start.8 = (bf16[2,128,512]{2,1,0:T(8,128)(2,1)S(1)}, bf16[2,128,512]{2,1,0:T(8,128)(2,1)S(1)}, u32[]{:S(2)}, u32[]{:S(2)}) collective-permute-start(bf16[2,128,512]{2,1,0:T(8,128)(2,1)S(1)} %get-tuple-element.19), channel_id=1, source_target_pairs={{0,4},{4,8},{8,12},{12,16},{16,20},{20,24},{24,28},{28,32},{32,36}... | collective-permute-start | bytes 786440 | tf_op jit(solution)/shard_map/ppermute | solution.py:14
  148.1 26.5 %copy-start.8 = (bf16[128,512]{1,0:T(8,128)(2,1)S(1)}, bf16[128,512]{1,0:T(8,128)(2,1)}, u32[]{:S(2)}) copy-start(bf16[128,512]{1,0:T(8,128)(2,1)} %copy-done.7) | copy-start | bytes 393220
  148.1 26.5 %copy-start.12 = (f32[128,512]{1,0:T(8,128)S(1)}, f32[128,512]{1,0:T(8,128)}, u32[]{:S(2)}) copy-start(f32[128,512]{1,0:T(8,128)} %get-tuple-element.16) | copy-start | bytes 786436
  148.1 27.2 %copy-start.3 = (bf16[1,640,512]{1,2,0:T(8,128)(2,1)S(1)}, bf16[1,640,512]{1,2,0:T(8,128)(2,1)}, u32[]{:S(2)}) copy-start(bf16[1,640,512]{1,2,0:T(8,128)(2,1)} %copy-done.2) | copy-start | bytes 1966084
  148.1 27.2 %copy-start.6 = (bf16[4,128,640]{1,2,0:T(8,128)(2,1)S(1)}, bf16[4,128,640]{1,2,0:T(8,128)(2,1)}, u32[]{:S(2)}) copy-start(bf16[4,128,640]{1,2,0:T(8,128)(2,1)} %fusion.5) | copy-start | bytes 1966084
  148.1 14.9 %collective-permute-start.10 = (bf16[2,128,512]{2,1,0:T(8,128)(2,1)S(1)}, bf16[2,128,512]{2,1,0:T(8,128)(2,1)S(1)}, u32[]{:S(2)}, u32[]{:S(2)}) collective-permute-start(bf16[2,128,512]{2,1,0:T(8,128)(2,1)S(1)} %get-tuple-element.20), channel_id=1, source_target_pairs={{4,0},{8,4},{12,8},{16,12},{20,16},{24,20},{28,24},{32,28},{36,32}... | collective-permute-start | bytes 786440 | tf_op jit(solution)/shard_map/ppermute | solution.py:14
  164.0 14.9 %collective-permute-start.9 = (bf16[2,128,512]{2,1,0:T(8,128)(2,1)}, bf16[2,128,512]{2,1,0:T(8,128)(2,1)}, u32[]{:S(2)}, u32[]{:S(2)}) collective-permute-start(bf16[2,128,512]{2,1,0:T(8,128)(2,1)} %get-tuple-element.17), channel_id=1, source_target_pairs={{0,4},{4,8},{8,12},{12,16},{16,20},{20,24},{24,28},{28,32},{32,36}... | collective-permute-start | bytes 786440 | tf_op jit(solution)/shard_map/ppermute | solution.py:14
  165.9 14.2 %collective-permute-start.11 = (bf16[2,128,512]{2,1,0:T(8,128)(2,1)}, bf16[2,128,512]{2,1,0:T(8,128)(2,1)}, u32[]{:S(2)}, u32[]{:S(2)}) collective-permute-start(bf16[2,128,512]{2,1,0:T(8,128)(2,1)} %get-tuple-element.18), channel_id=1, source_target_pairs={{4,0},{8,4},{12,8},{16,12},{20,16},{24,20},{28,24},{32,28},{36,32}... | collective-permute-start | bytes 786440 | tf_op jit(solution)/shard_map/ppermute | solution.py:14
  (12 other events, 98.8 us)
Sparse Core Ops, SparseCore 0:
  48.3 43.5 reduce-scatter.1
where the time goes:
time: 190 us; the launch traced here: 189 us
  starting transfers between devices  66.7 us (35%)
  waiting for transfers between devices  62.3 us (33%)
  between operations  14.7 us (8%)
  local copies, waits for them, and re-layouts  14.6 us (8%)
  blocking collectives  11.3 us (6%)
  other arithmetic  9.99 us (5%)
  matrix products  9.27 us (5%)
    ppermute x8, starting transfers between devices, shifted(): return lax.ppermute(block, axis, route)  46.3 us
    reduce_scatter x1, waiting for transfers between devices, per_device(): lax.psum_scatter(partial_out.astype(jnp.bfloat16), 'mp', scatter_dimensio...  41.9 us
    ppermute x8, waiting for transfers between devices, shifted(): return lax.ppermute(block, axis, route)  18.6 us
    ppermute x2, starting transfers between devices, with_halo(): lax.ppermute(lax.slice_in_dim(block, 0, width, axis=dim), axis, backward)  14.9 us
    all_gather x1, blocking collectives, per_device(): lax.all_gather(grad_input, 'mp', axis=1, tiled=True)  11.3 us
    ppermute x2, starting transfers between devices, with_halo(): lax.ppermute(lax.slice_in_dim(block, block.shape[dim] - width, None, axis...  5.47 us
    another operation x2, local copies, waits for them, and re-layouts, per_device(): jnp.stack([key_parts.reshape(window_len, local_width), value_parts.reshap...  4.56 us
    unnamed x68, local copies, waits for them, and re-layouts  4.26 us
  transfers between devices with their start and end apart: 13, of which 10 were waited for; matrix products, arithmetic and copies ran while one was open for 3% of the time, Pallas kernels for 0%

commit v1 on v0

--- a/solution.py
+++ b/solution.py
@@ -108,7 +108,9 @@
     grad_input = grad_hidden.astype(jnp.bfloat16)
     upstream = jnp.einsum(
         "rn,wn->rw",
-        lax.all_gather(grad_input, "mp", axis=1, tiled=True),
+        jnp.concatenate(
+            lax.all_to_all(jnp.stack([grad_input] * lax.axis_size("mp")), "mp", 0, 0), axis=1
+        ),
         out_weight,
         preferred_element_type=jnp.float32,
     ).astype(jnp.bfloat16)

time: 190 us -> 200 us (1.053)
  the two profiles are of different devices: /device:TPU:8 before, /device:TPU:24 now
where the time goes in v1:
time: 200 us; the launch traced here: 199 us
  starting transfers between devices  69.6 us (35%)
  waiting for transfers between devices  58.7 us (29%)
  blocking collectives  20 us (10%)
  local copies, waits for them, and re-layouts  16.4 us (8%)
  between operations  14.7 us (7%)
  other arithmetic  10 us (5%)
  matrix products  9.28 us (5%)
    ppermute x8, starting transfers between devices, shifted(): return lax.ppermute(block, axis, route)  47.7 us
    reduce_scatter x1, waiting for transfers between devices, per_device(): lax.psum_scatter(partial_out.astype(jnp.bfloat16), 'mp', scatter_dimensio...  39.2 us
    all_to_all x1, blocking collectives, per_device(): lax.all_to_all(jnp.stack([grad_input] * lax.axis_size('mp')), 'mp', 0, 0)  20 us
    ppermute x8, waiting for transfers between devices, shifted(): return lax.ppermute(block, axis, route)  17.6 us
    ppermute x2, starting transfers between devices, with_halo(): lax.ppermute(lax.slice_in_dim(block, 0, width, axis=dim), axis, backward)  16.4 us
    ppermute x2, starting transfers between devices, with_halo(): lax.ppermute(lax.slice_in_dim(block, block.shape[dim] - width, None, axis...  5.48 us
    another operation x2, local copies, waits for them, and re-layouts, per_device(): jnp.stack([key_parts.reshape(window_len, local_width), value_parts.reshap...  4.58 us
    unnamed x70, local copies, waits for them, and re-layouts  4.28 us
  transfers between devices with their start and end apart: 13, of which 10 were waited for; matrix products, arithmetic and copies ran while one was open for 3% of the time, Pallas kernels for 0%

profile of v1, /device:TPU:24, one launch (start us, length us, event | category | flops | bytes accessed | tf_op | source)
XLA Modules:
  0.0 198.7 jit_solution(3512670142833875977)
XLA Ops:
  9.5 4.3 %collective-permute-start = (bf16[2,128,512]{1,2,0:T(8,128)(2,1)S(1)}, bf16[2,128,512]{1,2,0:T(8,128)(2,1)S(1)}, u32[]{:S(2)}, u32[]{:S(2)}) collective-permute-start(bf16[2,128,512]{1,2,0:T(8,128)(2,1)S(1)} %pad_maximum_fusion.1), channel_id=1, source_target_pairs={{0,4},{4,8},{8,12},{12,16},{16,20},{20,24},{24,28},{28,32},{32,36}... | collective-permute-start | bytes 786440 | tf_op jit(solution)/shard_map/ppermute | solution.py:14
  13.7 10.7 %collective-permute-start.2 = (bf16[2,128,512]{1,2,0:T(8,128)(2,1)S(1)}, bf16[2,128,512]{1,2,0:T(8,128)(2,1)S(1)}, u32[]{:S(2)}, u32[]{:S(2)}) collective-permute-start(bf16[2,128,512]{1,2,0:T(8,128)(2,1)S(1)} %pad_maximum_fusion.1), channel_id=1, source_target_pairs={{4,0},{8,4},{12,8},{16,12},{20,16},{24,20},{28,24},{32,28},{36,32}... | collective-permute-start | bytes 786440 | tf_op jit(solution)/shard_map/ppermute | solution.py:14
  24.4 4.4 %collective-permute-done = bf16[2,128,512]{1,2,0:T(8,128)(2,1)S(1)} collective-permute-done((bf16[2,128,512]{1,2,0:T(8,128)(2,1)S(1)}, bf16[2,128,512]{1,2,0:T(8,128)(2,1)S(1)}, u32[]{:S(2)}, u32[]{:S(2)}) %collective-permute-start) | collective-permute-done | bytes 262176 | tf_op jit(solution)/shard_map/ppermute | solution.py:14
  28.8 1.9 collective-permute-start.1
  31.8 8.1 %collective-permute-start.3 = (bf16[2,128,512]{1,2,0:T(8,128)(2,1)S(1)}, bf16[2,128,512]{1,2,0:T(8,128)(2,1)S(1)}, u32[]{:S(2)}, u32[]{:S(2)}) collective-permute-start(bf16[2,128,512]{1,2,0:T(8,128)(2,1)S(1)} %collective-permute-done.2), channel_id=1, source_target_pairs={{4,0},{8,4},{12,8},{16,12},{20,16},{24,20},{28,24},{32,28},{36,32}... | collective-permute-start | bytes 786440 | tf_op jit(solution)/shard_map/ppermute | solution.py:14
  39.9 2.5 %collective-permute-done.1 = bf16[2,128,512]{1,2,0:T(8,128)(2,1)S(1)} collective-permute-done((bf16[2,128,512]{1,2,0:T(8,128)(2,1)S(1)}, bf16[2,128,512]{1,2,0:T(8,128)(2,1)S(1)}, u32[]{:S(2)}, u32[]{:S(2)}) %collective-permute-start.1) | collective-permute-done | bytes 262176 | tf_op jit(solution)/shard_map/ppermute | solution.py:14
  42.6 2.0 %collective-permute-done.3 = bf16[2,128,512]{1,2,0:T(8,128)(2,1)S(1)} collective-permute-done((bf16[2,128,512]{1,2,0:T(8,128)(2,1)S(1)}, bf16[2,128,512]{1,2,0:T(8,128)(2,1)S(1)}, u32[]{:S(2)}, u32[]{:S(2)}) %collective-permute-start.3) | collective-permute-done | bytes 262176 | tf_op jit(solution)/shard_map/ppermute | solution.py:14
  46.9 1.3 convolution_convert_fusion
  48.2 1.8 fusion.96
  50.0 39.2 %reduce-scatter.2.cloned.1.call-done = bf16[128,512]{1,0:T(8,128)(2,1)} async-done(((bf16[128,2048]{1,0:T(8,128)(2,1)}), bf16[128,512]{1,0:T(8,128)(2,1)}) %reduce-scatter.2.cloned.1.call-update) | async-done | bytes 131088 | tf_op jit(solution)/shard_map/reduce_scatter | solution.py:84
  90.2 3.6 %collective-permute-start.4 = (bf16[15,512]{1,0:T(8,128)(2,1)S(1)}, bf16[15,512]{1,0:T(8,128)(2,1)S(1)}, u32[]{:S(2)}, u32[]{:S(2)}) collective-permute-start(bf16[15,512]{1,0:T(8,128)(2,1)S(1)} %get-tuple-element.27), channel_id=1, source_target_pairs={{0,4},{4,8},{8,12},{12,16},{16,20},{20,24},{24,28},{28,32},{32,36}... | collective-permute-start | bytes 46088 | tf_op jit(solution)/shard_map/ppermute | solution.py:22
  93.8 8.0 %collective-permute-start.5 = (bf16[15,512]{1,0:T(8,128)(2,1)S(1)}, bf16[15,512]{1,0:T(8,128)(2,1)S(1)}, u32[]{:S(2)}, u32[]{:S(2)}) collective-permute-start(bf16[15,512]{1,0:T(8,128)(2,1)S(1)} %get-tuple-element.28), channel_id=1, source_target_pairs={{4,0},{8,4},{12,8},{16,12},{20,16},{24,20},{28,24},{32,28},{36,32}... | collective-permute-start | bytes 46088 | tf_op jit(solution)/shard_map/ppermute | solution.py:25
  103.5 2.3 %fusion.17 = (bf16[128,512]{1,0:T(8,128)(2,1)S(1)}, f32[128,512]{1,0:T(8,128)}) fusion(bf16[128,512]{1,0:T(8,128)(2,1)S(1)} %copy-done.14, f32[158,512]{1,0:T(8,128)S(1)} %maximum_convert_fusion, f32[512]{0:T(512)S(1)} %bitcast.150, f32[512]{0:T(512)S(1)} %bitcast.152, f32[512]{0:T(512)S(1)} %bitcast.94, f32[512]{0:T(512)S(1)} %bitcast.96, f32[512]{0:T(512)} %bitcast.98, ...), kind=kLoop, calls=%fused_computation.34 | loop fusion | flops 4653056 | bytes 8714240 | tf_op jit(solution)/shard_map/convert_element_type | solution.py:100
  105.8 1.9 collective-permute-start.6
  107.7 8.4 %collective-permute-start.7 = (bf16[15,512]{1,0:T(8,128)(2,1)S(1)}, bf16[15,512]{1,0:T(8,128)(2,1)S(1)}, u32[]{:S(2)}, u32[]{:S(2)}) collective-permute-start(bf16[15,512]{1,0:T(8,128)(2,1)S(1)} %get-tuple-element.26), channel_id=1, source_target_pairs={{4,0},{8,4},{12,8},{16,12},{20,16},{24,20},{28,24},{32,28},{36,32}... | collective-permute-start | bytes 46088 | tf_op jit(solution)/shard_map/ppermute | solution.py:25
  116.1 1.4 collective-permute-done.7
  120.3 20.0 %all_to_all.5 = bf16[4,128,512]{1,2,0:T(8,128)(2,1)S(1)} all-to-all(bf16[4,128,512]{1,2,0:T(8,128)(2,1)S(1)} %stack.22), channel_id=1, replica_groups=mesh['ctx'=128,'mp'=4] {'mp'}, dimensions={0} | all-to-all | bytes 1048576 | tf_op jit(solution)/shard_map/all_to_all | solution.py:112
  140.4 1.5 convolution_convert_fusion.1
  143.9 1.5 fusion.80
  145.4 1.3 fusion.5
  146.7 1.7 copy.42
  148.5 2.5 %fusion.99 = f32[4,640,128]{1,2,0:T(8,128)} fusion(bf16[4,128,640]{1,2,0:T(8,128)(2,1)} %fusion.5, bf16[128,4,128]{0,2,1:T(8,128)(2,1)S(1)} %bitcast.85), kind=kOutput, calls=%fused_computation.194 | convolution fusion | flops 83886080 | bytes 2097152 | tf_op jit(solution)/shard_map/hqk,qhd->khd/dot_general | solution.py:127
  151.0 2.8 %copy.41 = f32[1,640,512]{2,1,0:T(8,128)} copy(f32[1,640,512]{1,2,0:T(8,128)} %bitcast.80) | data formatting | bytes 2621440 | tf_op jit(solution)/shard_map/stack;reshape | solution.py:133
  153.8 1.6 fusion
  155.5 1.9 collective-permute-start.8
  157.5 10.3 %collective-permute-start.10 = (bf16[2,128,512]{2,1,0:T(8,128)(2,1)S(1)}, bf16[2,128,512]{2,1,0:T(8,128)(2,1)S(1)}, u32[]{:S(2)}, u32[]{:S(2)}) collective-permute-start(bf16[2,128,512]{2,1,0:T(8,128)(2,1)S(1)} %get-tuple-element.20), channel_id=1, source_target_pairs={{4,0},{8,4},{12,8},{16,12},{20,16},{24,20},{28,24},{32,28},{36,32}... | collective-permute-start | bytes 786440 | tf_op jit(solution)/shard_map/ppermute | solution.py:14
  167.7 4.3 %collective-permute-done.8 = bf16[2,128,512]{2,1,0:T(8,128)(2,1)S(1)} collective-permute-done((bf16[2,128,512]{2,1,0:T(8,128)(2,1)S(1)}, bf16[2,128,512]{2,1,0:T(8,128)(2,1)S(1)}, u32[]{:S(2)}, u32[]{:S(2)}) %collective-permute-start.8) | collective-permute-done | bytes 262176 | tf_op jit(solution)/shard_map/ppermute | solution.py:14
  172.0 1.4 collective-permute-done.10
  174.3 1.9 collective-permute-start.9
  176.2 8.6 %collective-permute-start.11 = (bf16[2,128,512]{2,1,0:T(8,128)(2,1)}, bf16[2,128,512]{2,1,0:T(8,128)(2,1)}, u32[]{:S(2)}, u32[]{:S(2)}) collective-permute-start(bf16[2,128,512]{2,1,0:T(8,128)(2,1)} %get-tuple-element.18), channel_id=1, source_target_pairs={{4,0},{8,4},{12,8},{16,12},{20,16},{24,20},{28,24},{32,28},{36,32}... | collective-permute-start | bytes 786440 | tf_op jit(solution)/shard_map/ppermute | solution.py:14
  186.7 2.0 %collective-permute-done.9 = bf16[2,128,512]{2,1,0:T(8,128)(2,1)} collective-permute-done((bf16[2,128,512]{2,1,0:T(8,128)(2,1)}, bf16[2,128,512]{2,1,0:T(8,128)(2,1)}, u32[]{:S(2)}, u32[]{:S(2)}) %collective-permute-start.9) | collective-permute-done | bytes 262176 | tf_op jit(solution)/shard_map/ppermute | solution.py:14
  189.9 1.2 fusion.10
  (103 shorter events, 17.7 us)
Async XLA Ops:
  7.2 39.8 %copy-start = (bf16[512,2048]{1,0:T(8,128)(2,1)S(1)}, bf16[512,2048]{1,0:T(8,128)(2,1)}, u32[]{:S(2)}) copy-start(bf16[512,2048]{1,0:T(8,128)(2,1)} %param.11) | copy-start | bytes 6291460
  7.2 82.0 %reduce-scatter.2.cloned.1.call-start = ((), (), s32[]{:S(2)}) async-start(), calls=%async_computation.2 | async-start | bytes 655360 | tf_op jit(solution)/shard_map/reduce_scatter | solution.py:84
  9.5 19.3 %collective-permute-start = (bf16[2,128,512]{1,2,0:T(8,128)(2,1)S(1)}, bf16[2,128,512]{1,2,0:T(8,128)(2,1)S(1)}, u32[]{:S(2)}, u32[]{:S(2)}) collective-permute-start(bf16[2,128,512]{1,2,0:T(8,128)(2,1)S(1)} %pad_maximum_fusion.1), channel_id=1, source_target_pairs={{0,4},{4,8},{8,12},{12,16},{16,20},{20,24},{24,28},{28,32},{32,36}... | collective-permute-start | bytes 786440 | tf_op jit(solution)/shard_map/ppermute | solution.py:14
  13.7 18.0 %collective-permute-start.2 = (bf16[2,128,512]{1,2,0:T(8,128)(2,1)S(1)}, bf16[2,128,512]{1,2,0:T(8,128)(2,1)S(1)}, u32[]{:S(2)}, u32[]{:S(2)}) collective-permute-start(bf16[2,128,512]{1,2,0:T(8,128)(2,1)S(1)} %pad_maximum_fusion.1), channel_id=1, source_target_pairs={{4,0},{8,4},{12,8},{16,12},{20,16},{24,20},{28,24},{32,28},{36,32}... | collective-permute-start | bytes 786440 | tf_op jit(solution)/shard_map/ppermute | solution.py:14
  28.8 13.6 %collective-permute-start.1 = (bf16[2,128,512]{1,2,0:T(8,128)(2,1)S(1)}, bf16[2,128,512]{1,2,0:T(8,128)(2,1)S(1)}, u32[]{:S(2)}, u32[]{:S(2)}) collective-permute-start(bf16[2,128,512]{1,2,0:T(8,128)(2,1)S(1)} %collective-permute-done), channel_id=1, source_target_pairs={{0,4},{4,8},{8,12},{12,16},{16,20},{20,24},{24,28},{28,32},{32,36}... | collective-permute-start | bytes 786440 | tf_op jit(solution)/shard_map/ppermute | solution.py:14
  31.8 12.9 %collective-permute-start.3 = (bf16[2,128,512]{1,2,0:T(8,128)(2,1)S(1)}, bf16[2,128,512]{1,2,0:T(8,128)(2,1)S(1)}, u32[]{:S(2)}, u32[]{:S(2)}) collective-permute-start(bf16[2,128,512]{1,2,0:T(8,128)(2,1)S(1)} %collective-permute-done.2), channel_id=1, source_target_pairs={{4,0},{8,4},{12,8},{16,12},{20,16},{24,20},{28,24},{32,28},{36,32}... | collective-permute-start | bytes 786440 | tf_op jit(solution)/shard_map/ppermute | solution.py:14
  48.2 55.1 %copy-start.14 = (bf16[128,512]{1,0:T(8,128)(2,1)S(1)}, bf16[128,512]{1,0:T(8,128)(2,1)}, u32[]{:S(2)}) copy-start(bf16[128,512]{1,0:T(8,128)(2,1)} %param.13) | copy-start | bytes 393220
  90.2 12.6 %collective-permute-start.4 = (bf16[15,512]{1,0:T(8,128)(2,1)S(1)}, bf16[15,512]{1,0:T(8,128)(2,1)S(1)}, u32[]{:S(2)}, u32[]{:S(2)}) collective-permute-start(bf16[15,512]{1,0:T(8,128)(2,1)S(1)} %get-tuple-element.27), channel_id=1, source_target_pairs={{0,4},{4,8},{8,12},{12,16},{16,20},{20,24},{24,28},{28,32},{32,36}... | collective-permute-start | bytes 46088 | tf_op jit(solution)/shard_map/ppermute | solution.py:22
  93.8 9.4 %collective-permute-start.5 = (bf16[15,512]{1,0:T(8,128)(2,1)S(1)}, bf16[15,512]{1,0:T(8,128)(2,1)S(1)}, u32[]{:S(2)}, u32[]{:S(2)}) collective-permute-start(bf16[15,512]{1,0:T(8,128)(2,1)S(1)} %get-tuple-element.28), channel_id=1, source_target_pairs={{4,0},{8,4},{12,8},{16,12},{20,16},{24,20},{28,24},{32,28},{36,32}... | collective-permute-start | bytes 46088 | tf_op jit(solution)/shard_map/ppermute | solution.py:25
  103.3 14.3 %copy-start.15 = (bf16[128,512]{1,0:T(8,128)(2,1)S(1)}, bf16[128,512]{1,0:T(8,128)(2,1)}, u32[]{:S(2)}) copy-start(bf16[128,512]{1,0:T(8,128)(2,1)} %param.13) | copy-start | bytes 393220
  103.3 14.3 %copy-start.16 = (f32[1,512]{1,0:T(1,128)S(1)}, f32[1,512]{1,0:T(1,128)}, u32[]{:S(2)}) copy-start(f32[1,512]{1,0:T(1,128)} %get-tuple-element.32) | copy-start | bytes 6148
  103.3 14.3 %copy-start.17 = (f32[1,512]{1,0:T(1,128)S(1)}, f32[1,512]{1,0:T(1,128)}, u32[]{:S(2)}) copy-start(f32[1,512]{1,0:T(1,128)} %get-tuple-element.33) | copy-start | bytes 6148
  103.3 14.3 %copy-start.18 = (f32[1,512]{1,0:T(1,128)S(1)}, f32[1,512]{1,0:T(1,128)}, u32[]{:S(2)}) copy-start(f32[1,512]{1,0:T(1,128)} %get-tuple-element.34) | copy-start | bytes 6148
  103.3 14.3 %copy-start.19 = (f32[1,512]{1,0:T(1,128)S(1)}, f32[1,512]{1,0:T(1,128)}, u32[]{:S(2)}) copy-start(f32[1,512]{1,0:T(1,128)} %get-tuple-element.35) | copy-start | bytes 6148
  103.4 14.3 %copy-start.20 = (f32[1,512]{1,0:T(1,128)S(1)}, f32[1,512]{1,0:T(1,128)}, u32[]{:S(2)}) copy-start(f32[1,512]{1,0:T(1,128)} %get-tuple-element.36) | copy-start | bytes 6148
  103.4 14.3 %copy-start.21 = (f32[1,512]{1,0:T(1,128)S(1)}, f32[1,512]{1,0:T(1,128)}, u32[]{:S(2)}) copy-start(f32[1,512]{1,0:T(1,128)} %get-tuple-element.37) | copy-start | bytes 6148
  103.4 14.3 %copy-start.22 = (f32[1,512]{1,0:T(1,128)S(1)}, f32[1,512]{1,0:T(1,128)}, u32[]{:S(2)}) copy-start(f32[1,512]{1,0:T(1,128)} %get-tuple-element.38) | copy-start | bytes 6148
  103.4 14.3 %copy-start.23 = (f32[1,512]{1,0:T(1,128)S(1)}, f32[1,512]{1,0:T(1,128)}, u32[]{:S(2)}) copy-start(f32[1,512]{1,0:T(1,128)} %get-tuple-element.39) | copy-start | bytes 6148
  103.4 14.3 %copy-start.24 = (f32[1,512]{1,0:T(1,128)S(1)}, f32[1,512]{1,0:T(1,128)}, u32[]{:S(2)}) copy-start(f32[1,512]{1,0:T(1,128)} %get-tuple-element.40) | copy-start | bytes 6148
  103.4 14.3 %copy-start.25 = (f32[1,512]{1,0:T(1,128)S(1)}, f32[1,512]{1,0:T(1,128)}, u32[]{:S(2)}) copy-start(f32[1,512]{1,0:T(1,128)} %get-tuple-element.41) | copy-start | bytes 6148
  105.8 10.4 %collective-permute-start.6 = (bf16[15,512]{1,0:T(8,128)(2,1)S(1)}, bf16[15,512]{1,0:T(8,128)(2,1)S(1)}, u32[]{:S(2)}, u32[]{:S(2)}) collective-permute-start(bf16[15,512]{1,0:T(8,128)(2,1)S(1)} %get-tuple-element.25), channel_id=1, source_target_pairs={{0,4},{4,8},{8,12},{12,16},{16,20},{20,24},{24,28},{28,32},{32,36}... | collective-permute-start | bytes 46088 | tf_op jit(solution)/shard_map/ppermute | solution.py:22
  107.7 9.9 %collective-permute-start.7 = (bf16[15,512]{1,0:T(8,128)(2,1)S(1)}, bf16[15,512]{1,0:T(8,128)(2,1)S(1)}, u32[]{:S(2)}, u32[]{:S(2)}) collective-permute-start(bf16[15,512]{1,0:T(8,128)(2,1)S(1)} %get-tuple-element.26), channel_id=1, source_target_pairs={{4,0},{8,4},{12,8},{16,12},{20,16},{24,20},{28,24},{32,28},{36,32}... | collective-permute-start | bytes 46088 | tf_op jit(solution)/shard_map/ppermute | solution.py:25
  118.6 21.8 %copy-start.13 = (bf16[128,512]{1,0:T(8,128)(2,1)}, bf16[128,512]{1,0:T(8,128)(2,1)S(1)}, u32[]{:S(2)}) copy-start(bf16[128,512]{1,0:T(8,128)(2,1)S(1)} %fusion.44) | copy-start | bytes 393220
  153.8 19.5 %copy-start.1 = (f32[1,640,512]{2,1,0:T(8,128)S(1)}, f32[1,640,512]{2,1,0:T(8,128)}, u32[]{:S(2)}) copy-start(f32[1,640,512]{2,1,0:T(8,128)} %copy.41) | copy-start | bytes 3932164
  155.5 16.5 %collective-permute-start.8 = (bf16[2,128,512]{2,1,0:T(8,128)(2,1)S(1)}, bf16[2,128,512]{2,1,0:T(8,128)(2,1)S(1)}, u32[]{:S(2)}, u32[]{:S(2)}) collective-permute-start(bf16[2,128,512]{2,1,0:T(8,128)(2,1)S(1)} %get-tuple-element.19), channel_id=1, source_target_pairs={{0,4},{4,8},{8,12},{12,16},{16,20},{20,24},{24,28},{28,32},{32,36}... | collective-permute-start | bytes 786440 | tf_op jit(solution)/shard_map/ppermute | solution.py:14
  157.4 27.4 %copy-start.8 = (bf16[128,512]{1,0:T(8,128)(2,1)S(1)}, bf16[128,512]{1,0:T(8,128)(2,1)}, u32[]{:S(2)}) copy-start(bf16[128,512]{1,0:T(8,128)(2,1)} %copy-done.7) | copy-start | bytes 393220
  157.4 27.4 %copy-start.12 = (f32[128,512]{1,0:T(8,128)S(1)}, f32[128,512]{1,0:T(8,128)}, u32[]{:S(2)}) copy-start(f32[128,512]{1,0:T(8,128)} %get-tuple-element.16) | copy-start | bytes 786436
  157.4 28.2 %copy-start.3 = (bf16[1,640,512]{1,2,0:T(8,128)(2,1)S(1)}, bf16[1,640,512]{1,2,0:T(8,128)(2,1)}, u32[]{:S(2)}) copy-start(bf16[1,640,512]{1,2,0:T(8,128)(2,1)} %copy-done.2) | copy-start | bytes 1966084
  157.4 28.2 %copy-start.6 = (bf16[4,128,640]{1,2,0:T(8,128)(2,1)S(1)}, bf16[4,128,640]{1,2,0:T(8,128)(2,1)}, u32[]{:S(2)}) copy-start(bf16[4,128,640]{1,2,0:T(8,128)(2,1)} %fusion.5) | copy-start | bytes 1966084
  157.5 15.9 %collective-permute-start.10 = (bf16[2,128,512]{2,1,0:T(8,128)(2,1)S(1)}, bf16[2,128,512]{2,1,0:T(8,128)(2,1)S(1)}, u32[]{:S(2)}, u32[]{:S(2)}) collective-permute-start(bf16[2,128,512]{2,1,0:T(8,128)(2,1)S(1)} %get-tuple-element.20), channel_id=1, source_target_pairs={{4,0},{8,4},{12,8},{16,12},{20,16},{24,20},{28,24},{32,28},{36,32}... | collective-permute-start | bytes 786440 | tf_op jit(solution)/shard_map/ppermute | solution.py:14
  174.3 14.4 %collective-permute-start.9 = (bf16[2,128,512]{2,1,0:T(8,128)(2,1)}, bf16[2,128,512]{2,1,0:T(8,128)(2,1)}, u32[]{:S(2)}, u32[]{:S(2)}) collective-permute-start(bf16[2,128,512]{2,1,0:T(8,128)(2,1)} %get-tuple-element.17), channel_id=1, source_target_pairs={{0,4},{4,8},{8,12},{12,16},{16,20},{20,24},{24,28},{28,32},{32,36}... | collective-permute-start | bytes 786440 | tf_op jit(solution)/shard_map/ppermute | solution.py:14
  176.2 13.7 %collective-permute-start.11 = (bf16[2,128,512]{2,1,0:T(8,128)(2,1)}, bf16[2,128,512]{2,1,0:T(8,128)(2,1)}, u32[]{:S(2)}, u32[]{:S(2)}) collective-permute-start(bf16[2,128,512]{2,1,0:T(8,128)(2,1)} %get-tuple-element.18), channel_id=1, source_target_pairs={{4,0},{8,4},{12,8},{16,12},{20,16},{24,20},{28,24},{32,28},{36,32}... | collective-permute-start | bytes 786440 | tf_op jit(solution)/shard_map/ppermute | solution.py:14
  (13 other events, 117.7 us)
Sparse Core Ops, SparseCore 0:
  48.3 40.8 reduce-scatter.1
